TPU v7x, 256 devices: a whole 4x4x8 slice. The times are simulated.
256 devices in a mesh: facet: 16 (over x, y_lo, core), freq: 16 (over z, y_hi).
Axes of the slice: x: 4, y: 4 (y_hi: 2, y_lo: 2; y = y_hi * 2 + y_lo), z: 8, core: 2. Of those that a mesh axis runs over, the one named last changes fastest.
Arguments:
- residual: float32 [32, 16, 512, 512], P('freq', 'facet'), may hold values from -3 to 3
- components: bfloat16 [4, 32, 128, 128], P(None, 'freq', 'facet'), may hold values from -6 to 6
- chan_weight: float32 [32], P('freq'), may hold values from 0.3 to 3
- tile_pos: int32 [4, 2], replicated, may hold values from 0 to 1920, as said below
- facet_psf: int32 [16], P('facet'), may hold values from 0 to 3
- psf_spectra: bfloat16 [4, 32, 2, 768, 768], P(None, 'freq', None, 'facet'), may hold values from -48 to 48
Outputs:
- new_residual: float32 [32, 16, 512, 512], P('freq', 'facet')
Inputs may be any that keep to these rules, and one draw needn't show every extreme that they name: `tile_pos`: each row is a tile's top-left pixel (row, column); the row never exceeds 2048 - 128 and the column never exceeds 2048 - 128; some tile lies at the image's right edge and some tile at its top edge.
All inputs are finite; a program needn't handle non-finite values.
Results may differ from a plain program's by a relative error of at most 0.0045.
Values may be sent and summed in bfloat16 or wider, within the bound.
A program may use at most 128 MiB of HBM per device.

v0:
```python
import functools
import math

import jax
import jax.numpy as jnp
import ml_dtypes
import numpy as np
from jax import lax
from jax.experimental import pallas as pl
from jax.experimental.pallas import tpu as pltpu
from jax.sharding import PartitionSpec as P

CHAN = 32
FS = 512
PAD = 128
TS = 128
NTILE = 4
FCOLS = 4
FRAME = 768
N = 16
ROWS = 48
SLOTS = 24
MIB = 1 << 20
MESH = pl.DeviceIdType.MESH
VMEM = pl.BlockSpec(memory_space=pltpu.VMEM)
SMEM = pl.BlockSpec(memory_space=pltpu.SMEM)
f32 = jnp.float32
bf16 = jnp.bfloat16


def own_row(m, slot):
    return 0 if slot == 0 and m >= N // 2 else SLOTS + slot


def angles(left, right):
    return (left * right % FRAME).astype(np.float64) * (2.0 * math.pi / FRAME)


def half(table):
    return table.astype(ml_dtypes.bfloat16)


@functools.cache
def tables():
    slot_of = np.arange(4)[:, None, None] * 8 + np.arange(8)[None, None, :]
    slot_of = np.broadcast_to(slot_of, (4, 2, 8)).reshape(-1)
    chan_of = np.broadcast_to(np.arange(2)[None, :, None], (4, 2, 8)).reshape(-1)
    k_rows = np.zeros((N, 64), np.int64)
    own = np.zeros((N, 48, 96))
    mirror = np.zeros((48, 96))
    for m in range(N):
        for r in range(48):
            k_rows[m, r] = ROWS * m + own_row(m, slot_of[r])
            own[m, r, chan_of[r] * ROWS + own_row(m, slot_of[r])] = 1.0
    for r in range(48):
        mirror[r, chan_of[r] * ROWS + SLOTS - slot_of[r]] = 1.0
    tile_rows = np.arange(N)[:, None, None] * 8 + np.arange(8)[None, None, :]
    tile_rows = np.broadcast_to(tile_rows, (N, 2, 8)).reshape(-1)
    tile_chan = np.broadcast_to(np.arange(2)[None, :, None], (N, 2, 8)).reshape(-1)
    theta = angles(k_rows[:, :, None], tile_rows[None, None, :])
    same = (chan_of[:, None] == tile_chan[None, :])[None]
    rows = np.concatenate([np.cos(theta) * same, -np.sin(theta) * same], axis=1)
    theta = angles(np.arange(TS)[:, None], np.arange(FRAME)[None, :])
    cos, sin = np.cos(theta), np.sin(theta)
    cols = np.block([[cos, -sin], [sin, cos]])
    theta = angles(np.arange(FRAME)[:, None], PAD + np.arange(FS)[None, :])
    cos, sin = np.cos(theta), np.sin(theta)
    back_cols = np.block([[cos, sin], [-sin, cos]])
    back_rows = np.zeros((FS, N, 2, SLOTS))
    y = PAD + np.arange(FS)
    for m in range(N):
        for slot in range(SLOTS):
            theta = angles(np.int64(ROWS * m + own_row(m, slot)), y)
            back_rows[:, m, 0, slot] = np.cos(theta)
            back_rows[:, m, 1, slot] = -np.sin(theta)
    back_rows[:, N // 2, 0, 0] *= 0.5
    back_rows[:, N // 2, 1, 0] = 0.5
    flip = np.zeros((FRAME, FRAME))
    flip[(FRAME - np.arange(FRAME)) % FRAME, np.arange(FRAME)] = 1.0
    return dict(
        k_rows=k_rows.astype(np.int32),
        own=half(own),
        mirror=half(mirror),
        rows=half(rows),
        cols=half(cols),
        back_cols=half(back_cols),
        back_rows=half(back_rows.reshape(FS, N * 2 * SLOTS)),
        flip=half(flip),
    )


def channel_at(index):
    return (2 * index - (CHAN - 1)).astype(f32) * (1.0 / CHAN)


def exchange_kernel(
    comps_ref, weight_ref, psf_of_ref, psf_ref, row0_ref, mirror_ref,
    model_ref, far_ref, far0_ref,
    send_a, recv_a, send_b, send_m,
    a_send, a_recv, b_send, b_recv, m_send, m_recv,
):
    facet = lax.axis_index("facet")
    freq = lax.axis_index("freq")
    barrier = pltpu.get_barrier_semaphore()

    def greet(d, _):
        pl.semaphore_signal(barrier, inc=1, device_id={"freq": (freq + d) % N}, device_id_type=MESH)
        pl.semaphore_signal(barrier, inc=1, device_id={"facet": (facet + d) % N}, device_id_type=MESH)
        return 0

    lax.fori_loop(1, N, greet, 0)

    send_a[0:64, :] = comps_ref[...]
    row = lax.broadcasted_iota(jnp.int32, (8, 128), 0)
    parts = []
    for c in range(2):
        whole = jnp.full((8, 128), weight_ref[c], f32)
        first = whole.astype(bf16).astype(f32)
        second = (whole - first).astype(bf16).astype(f32)
        third = (whole - first) - second
        parts.append(jnp.where(row == 0, first, jnp.where(row == 1, second, jnp.where(row == 2, third, 0.0))))
    send_a[64:80, :] = jnp.concatenate(parts, axis=0).astype(bf16)
    pl.semaphore_wait(barrier, 2 * (N - 1))

    def copy_a(d, slot):
        return pltpu.make_async_remote_copy(
            src_ref=send_a, dst_ref=recv_a.at[slot], send_sem=a_send.at[d], recv_sem=a_recv.at[slot],
            device_id={"freq": (freq + d) % N}, device_id_type=MESH,
        )

    def copy_b(d, slot):
        return pltpu.make_async_remote_copy(
            src_ref=send_b, dst_ref=model_ref.at[slot], send_sem=b_send.at[d], recv_sem=b_recv.at[slot],
            device_id={"facet": (facet + d) % N}, device_id_type=MESH,
        )

    def start_a(d, _):
        copy_a(d, freq).start()
        return 0

    lax.fori_loop(1, N, start_a, 0)
    recv_a[freq] = send_a[...]

    for index in range(8):
        both = psf_ref[index // 2, :, index % 2].reshape(2 * ROWS, FRAME)
        send_m[index] = jnp.dot(mirror_ref[...], both, preferred_element_type=f32).astype(bf16)
    copy_m = pltpu.make_async_remote_copy(
        src_ref=send_m, dst_ref=far_ref, send_sem=m_send.at[0], recv_sem=m_recv.at[0],
        device_id={"facet": N - 1 - facet}, device_id_type=MESH,
    )
    copy_m.start()
    is_first = 1 - (facet + N - 1) // N
    is_middle = 1 - ((facet + N // 2) % N + N - 1) // N
    copy_0 = pltpu.make_async_remote_copy(
        src_ref=row0_ref, dst_ref=far0_ref, send_sem=m_send.at[1], recv_sem=m_recv.at[1],
        device_id={"facet": (N - facet) % N + (N // 2) * (is_first - is_middle)}, device_id_type=MESH,
    )
    copy_0.start()

    def land_a(d, _):
        copy_a(d, (freq + N - d) % N).wait_recv()
        return 0

    lax.fori_loop(1, N, land_a, 0)

    def add(q, total):
        total = list(total)
        block = recv_a[q].astype(f32)
        comp = block[0:64].reshape(NTILE, 2, 8, 128)
        for c in range(2):
            x = channel_at(2 * q + c)
            power = jnp.sum(block[64 + 8 * c : 72 + 8 * c], axis=0, keepdims=True)
            for j in range(5):
                if j < 3:
                    total[j] = total[j] + power * comp[:, c]
                total[3 + j] = total[3 + j] + power
                power = power * x
        return tuple(total)

    zeros = tuple(jnp.zeros((NTILE, 8, 128), f32) for _ in range(3)) + tuple(jnp.zeros((1, 128), f32) for _ in range(5))
    m0, m1, m2, g0, g1, g2, g3, g4 = lax.fori_loop(0, N, add, zeros)
    c00 = g2 * g4 - g3 * g3
    c01 = g2 * g3 - g1 * g4
    c02 = g1 * g3 - g2 * g2
    c11 = g0 * g4 - g2 * g2
    c12 = g1 * g2 - g0 * g3
    c22 = g0 * g2 - g1 * g1
    det = g0 * c00 + g1 * c01 + g2 * c02
    a0 = ((c00 * m0 + c01 * m1 + c02 * m2) / det).astype(bf16).astype(f32)
    a1 = ((c01 * m0 + c11 * m1 + c12 * m2) / det).astype(bf16).astype(f32)
    a2 = ((c02 * m0 + c12 * m1 + c22 * m2) / det).astype(bf16).astype(f32)
    both = []
    for c in range(2):
        x = channel_at(2 * freq + c)
        both.append(a0 + a1 * x + a2 * (x * x))
    send_b[0:64, :] = jnp.stack(both, axis=1).reshape(64, 128).astype(bf16)
    send_b[64:80, :] = jnp.full((16, 128), psf_of_ref[0].astype(f32), f32).astype(bf16)

    def start_b(d, _):
        copy_b(d, facet).start()
        return 0

    lax.fori_loop(1, N, start_b, 0)
    model_ref[facet] = send_b[...]

    def land_b(d, _):
        copy_b(d, (facet + N - d) % N).wait_recv()
        copy_a(d, freq).wait_send()
        copy_b(d, facet).wait_send()
        return 0

    lax.fori_loop(1, N, land_b, 0)
    copy_0.wait()
    copy_m.wait()


def exchange(comps, weight, psf_of, psf, row0, mirror):
    dma = pltpu.SemaphoreType.DMA
    return pl.pallas_call(
        exchange_kernel,
        out_shape=(
            jax.ShapeDtypeStruct((N, 80, 128), bf16),
            jax.ShapeDtypeStruct((8, 48, FRAME), bf16),
            jax.ShapeDtypeStruct((16, FRAME), bf16),
        ),
        in_specs=[VMEM, SMEM, SMEM, VMEM, VMEM, VMEM],
        out_specs=(VMEM, VMEM, VMEM),
        scratch_shapes=[
            pltpu.VMEM((80, 128), bf16),
            pltpu.VMEM((N, 80, 128), bf16),
            pltpu.VMEM((80, 128), bf16),
            pltpu.VMEM((8, 48, FRAME), bf16),
            dma((N,)), dma((N,)), dma((N,)), dma((N,)), dma((2,)), dma((2,)),
        ],
        compiler_params=pltpu.CompilerParams(collective_id=0, has_side_effects=True, vmem_limit_bytes=24 * MIB),
        name="exchange",
    )(comps, weight, psf_of, psf, row0, mirror)


def product_kernel(
    tile_pos_ref, model_ref, psf_ref, far_ref, far0_ref, own_ref, flip_ref, rows_ref, cols_ref, row_ph_ref, col_ph_ref,
    out_ref,
    psf_sum, back, tiles, spec,
):
    facet = lax.axis_index("facet")
    middle = facet == N // 2
    upper = facet >= N // 2

    for t in range(NTILE):
        model = model_ref[:, 16 * t : 16 * t + 16, :].reshape(256, 128)
        half_way = jnp.dot(rows_ref[...], model, preferred_element_type=f32).astype(bf16)
        half_way = jnp.concatenate([half_way[0:64], half_way[64:128]], axis=1)
        tiles[t] = jnp.dot(half_way, cols_ref[...], preferred_element_type=f32)

    row = lax.broadcasted_iota(jnp.int32, (16, FRAME), 0)
    for index in range(8):
        p, ri = index // 2, index % 2
        both = psf_ref[p, :, ri].reshape(2 * ROWS, FRAME)
        chosen = jnp.dot(own_ref[...], both, preferred_element_type=f32)
        psf_sum[p, ri, 0:48] = chosen
        zero_row = [far0_ref[4 * p + 2 * c + ri : 4 * p + 2 * c + ri + 1].astype(f32) for c in range(2)]
        zero_rows = jnp.where(row == 0, zero_row[0], jnp.where(row == 8, zero_row[1], 0.0))
        psf_sum[p, ri, 48:64] = zero_rows
        far = far_ref[index].astype(f32)
        lead = jnp.where((row % 8 == 0) & upper, jnp.where(middle, chosen[0:16], zero_rows), far[0:16])
        back[index, 0:16] = lead.astype(bf16)
        back[index, 16:48] = far_ref[index, 16:48]
        back[index, 48:64] = zero_rows.astype(bf16)
    for index in range(8):
        p, ri = index // 2, index % 2
        flipped = jnp.dot(back[index], flip_ref[...], preferred_element_type=f32)
        psf_sum[p, ri] = psf_sum[p, ri] + (flipped if ri == 0 else -flipped)

    lane = lax.broadcasted_iota(jnp.int32, (64, 128), 1)

    def one_facet(f, _):
        a, b = f // FCOLS, f % FCOLS
        counted = []
        for t in range(NTILE):
            oy = tile_pos_ref[t, 0] - a * FS + PAD
            ox = tile_pos_ref[t, 1] - b * FS + PAD
            counted.append((oy >= 0) & (oy <= FRAME - TS) & (ox >= 0) & (ox <= FRAME - TS))
        some = counted[0] | counted[1] | counted[2] | counted[3]

        @pl.when(jnp.logical_not(some))
        def _():
            out_ref[f] = jnp.zeros((48, 2 * FRAME), bf16)

        @pl.when(some)
        def _():
            spec[...] = jnp.zeros_like(spec)
            for t in range(NTILE):

                @pl.when(counted[t])
                def _():
                    at = t * FCOLS + a
                    rc = jnp.sum(jnp.where(lane == at, row_ph_ref[...], 0.0), axis=1, keepdims=True)
                    rs = jnp.sum(jnp.where(lane == at + 16, row_ph_ref[...], 0.0), axis=1, keepdims=True)
                    cc = col_ph_ref[0, pl.ds(t * FCOLS + b, 1), :]
                    cs = col_ph_ref[1, pl.ds(t * FCOLS + b, 1), :]

                    def group(g):
                        at = slice(16 * g, 16 * g + 16)
                        pr = rc[at] * cc - rs[at] * cs
                        pi = rc[at] * cs + rs[at] * cc
                        tr = tiles[t, at, 0:FRAME]
                        ti = tiles[t, at, FRAME : 2 * FRAME]
                        spec[0, at] = spec[0, at] + (pr * tr - pi * ti)
                        spec[1, at] = spec[1, at] + (pr * ti + pi * tr)

                    for g in range(3):
                        group(g)

                    @pl.when(middle)
                    def _():
                        group(3)

            psf = jnp.max(model_ref[f, 64:80, :].astype(f32)).astype(jnp.int32)

            def group(g):
                at = slice(16 * g, 16 * g + 16)
                sr, si = spec[0, at], spec[1, at]
                hr, hi = psf_sum[psf, 0, at], psf_sum[psf, 1, at]
                return sr * hr - si * hi, sr * hi + si * hr

            for g in range(3):
                re, im = group(g)
                out_ref[f, 16 * g : 16 * g + 16, 0:FRAME] = re.astype(bf16)
                out_ref[f, 16 * g : 16 * g + 16, FRAME : 2 * FRAME] = im.astype(bf16)

            @pl.when(middle)
            def _():
                re, im = group(0)
                more_re, more_im = group(3)
                out_ref[f, 0:16, 0:FRAME] = (re - more_im).astype(bf16)
                out_ref[f, 0:16, FRAME : 2 * FRAME] = (im + more_re).astype(bf16)

        return 0

    lax.fori_loop(0, N, one_facet, 0)


def products(*args):
    return pl.pallas_call(
        product_kernel,
        out_shape=jax.ShapeDtypeStruct((N, 48, 2 * FRAME), bf16),
        in_specs=[SMEM] + [VMEM] * 10,
        out_specs=VMEM,
        scratch_shapes=[
            pltpu.VMEM((4, 2, 64, FRAME), f32),
            pltpu.VMEM((8, 64, FRAME), bf16),
            pltpu.VMEM((NTILE, 64, 2 * FRAME), f32),
            pltpu.VMEM((2, 64, FRAME), f32),
        ],
        compiler_params=pltpu.CompilerParams(vmem_limit_bytes=24 * MIB),
        name="products",
    )(*args)


def columns_kernel(prod_ref, back_ref, out_ref, send, sent, landed):
    facet = lax.axis_index("facet")
    freq = lax.axis_index("freq")
    del freq
    barrier = pltpu.get_barrier_semaphore()

    def greet(d, _):
        pl.semaphore_signal(barrier, inc=1, device_id={"facet": (facet + d) % N}, device_id_type=MESH)
        return 0

    lax.fori_loop(1, N, greet, 0)

    def copy(to, slot):
        return pltpu.make_async_remote_copy(
            src_ref=send.at[to], dst_ref=out_ref.at[:, slot], send_sem=sent.at[to], recv_sem=landed.at[slot],
            device_id={"facet": to}, device_id_type=MESH,
        )

    mine = facet // FCOLS
    within = facet % FCOLS
    for step, shift in enumerate((2, 1, 3, 0)):
        a = (mine + shift) % FCOLS
        block = prod_ref[pl.ds(a * FCOLS, FCOLS)].reshape(FCOLS * 48, 2 * FRAME)
        w = jnp.dot(block, back_ref[...], preferred_element_type=f32)
        w = w.reshape(FCOLS, 3, 2, 8, 2 * FS)
        for b in range(FCOLS):
            for c in range(2):
                for ri in range(2):
                    part = w[b, :, c, :, ri * FS : (ri + 1) * FS].reshape(SLOTS, FS)
                    if ri == 0:
                        real = part
                send[a * FCOLS + b, c] = jnp.concatenate([real, part], axis=0).astype(bf16)
        if step == 0:
            pl.semaphore_wait(barrier, N - 1)
        for j in range(FCOLS):
            if shift == 0 and j == 0:
                continue
            copy(a * FCOLS + (within + j) % FCOLS, facet).start()
    for c in range(2):
        out_ref[c, facet] = send[facet, c]

    def land(d, _):
        copy((facet + N - d) % N, (facet + N - d) % N).wait()
        return 0

    lax.fori_loop(1, N, land, 0)


def columns(prod, back):
    dma = pltpu.SemaphoreType.DMA
    return pl.pallas_call(
        columns_kernel,
        out_shape=jax.ShapeDtypeStruct((2, N, 48, FS), bf16),
        in_specs=[VMEM, VMEM],
        out_specs=VMEM,
        scratch_shapes=[pltpu.VMEM((N, 2, 48, FS), bf16), dma((N,)), dma((N,))],
        compiler_params=pltpu.CompilerParams(collective_id=1, has_side_effects=True, vmem_limit_bytes=24 * MIB),
        name="columns",
    )(prod, back)


def rows_kernel(residual_ref, w_ref, back_ref, out_ref):
    convolved = jnp.dot(back_ref[...], w_ref[0], preferred_element_type=f32)
    out_ref[0, 0] = residual_ref[0, 0] - convolved * (1.0 / (FRAME * FRAME))


def subtract(residual, w, back):
    return pl.pallas_call(
        rows_kernel,
        grid=(2,),
        out_shape=jax.ShapeDtypeStruct(residual.shape, f32),
        in_specs=[
            pl.BlockSpec((1, 1, FS, FS), lambda c: (c, 0, 0, 0)),
            pl.BlockSpec((1, FRAME, FS), lambda c: (c, 0, 0)),
            pl.BlockSpec((FS, FRAME), lambda c: (0, 0)),
        ],
        out_specs=pl.BlockSpec((1, 1, FS, FS), lambda c: (c, 0, 0, 0)),
        compiler_params=pltpu.CompilerParams(vmem_limit_bytes=24 * MIB),
        name="subtract",
    )(residual, w, back)


def phases(products):
    theta = (products % FRAME).astype(f32) * (2.0 * math.pi / FRAME)
    return jnp.cos(theta), -jnp.sin(theta)


def shards(residual, components, chan_weight, tile_pos, facet_psf, psf_spectra):
    table = {name: jnp.asarray(value) for name, value in tables().items()}
    facet = lax.axis_index("facet")

    def mine(name):
        return lax.dynamic_index_in_dim(table[name], facet, 0, keepdims=False)

    anchors = jnp.arange(FCOLS, dtype=jnp.int32) * FS - PAD
    oy = (tile_pos[:, 0][:, None] - anchors).reshape(-1)
    ox = (tile_pos[:, 1][:, None] - anchors).reshape(-1)
    row_ph = jnp.concatenate(phases(mine("k_rows")[:, None] * oy[None, :]), axis=1)
    row_ph = jnp.pad(row_ph, ((0, 0), (0, 96)))
    col_ph = jnp.stack(phases(ox[:, None] * jnp.arange(FRAME, dtype=jnp.int32)[None, :]))
    model, far, far0 = exchange(
        components.reshape(64, 128), chan_weight, facet_psf, psf_spectra,
        psf_spectra[:, :, :, 0, :].reshape(16, FRAME), table["mirror"],
    )
    prod = products(
        tile_pos, model, psf_spectra, far, far0, mine("own"), table["flip"], mine("rows"), table["cols"], row_ph, col_ph,
    )
    w = columns(prod, table["back_cols"])
    return subtract(residual, w.reshape(2, FRAME, FS), table["back_rows"])


def solution(mesh):
    placed = (
        P("freq", "facet", None, None),
        P(None, "freq", "facet", None),
        P("freq"),
        P(),
        P("facet"),
        P(None, "freq", None, "facet", None),
    )
    return jax.shard_map(
        shards,
        mesh=mesh,
        in_specs=placed,
        out_specs=P("freq", "facet", None, None),
        check_vma=False,
    )
```

profile of v0, /device:TPU:1, one launch (start us, length us, event | category | flops | bytes accessed | tf_op | source)
XLA Modules:
  0.0 83.6 jit_solution(11729861072454181167)
XLA Ops:
  0.0 0.0 copy-start.6
  0.7 0.7 fusion.10
  1.4 0.8 slice_bitcast_fusion
  2.2 0.8 copy.18.tile_pos_ref
  3.0 0.1 broadcast_subtract_fusion
  3.0 0.1 sub.58
  3.1 0.1 sub.54
  3.2 0.1 fusion.6
  3.3 0.7 dynamic-slice_bitcast_fusion.1.own_ref
  4.0 0.1 copy.17
  4.1 1.1 %slice_reduce_fusion = bf16[4,2,2,768]{3,2,1,0:T(2,128)(2,1)S(1)} fusion(bf16[4,2,2,48,768]{4,3,2,1,0:T(8,128)(2,1)} %psf_ref.3), kind=kLoop, calls=%fused_computation.10 | loop fusion | bytes 49152 | tf_op jit(solution)/shard_map/slice | solution.py:462
  5.2 0.1 multiply_cosine_fusion
  5.3 0.1 select_maximum_fusion.row_ph_ref
  5.4 0.8 %dynamic-slice_bitcast_fusion.rows_ref = bf16[128,256]{1,0:T(8,128)(2,1)S(1)} fusion(bf16[16,128,256]{2,1,0:T(8,128)(2,1)} %constant.66.clone, s32[]{:T(128)S(6)} %select_n.32), kind=kLoop, calls=%fused_computation.2 | loop fusion | bytes 131076 | tf_op jit(solution)/shard_map/jit(dynamic_index_in_dim)/squeeze | solution.py:452
  6.2 0.3 fusion.4
  6.6 0.0 copy-start
  6.6 1.3 %copy-done = bf16[4,2,2,48,768]{4,3,2,1,0:T(8,128)(2,1)S(1)} copy-done((bf16[4,2,2,48,768]{4,3,2,1,0:T(8,128)(2,1)S(1)}, bf16[4,2,2,48,768]{4,3,2,1,0:T(8,128)(2,1)}, u32[]{:S(2)}) %copy-start) | copy-done | bytes 1179672
  7.8 0.0 copy-start.7
  7.8 0.7 copy-done.7
  8.5 0.0 copy-start.8
  8.5 0.7 copy-done.8
  9.2 0.0 copy-start.9
  9.3 0.7 copy-done.9
  9.9 38.7 %exchange.1 = (bf16[16,80,128]{2,1,0:T(8,128)(2,1)S(1)}, bf16[8,48,768]{2,1,0:T(8,128)(2,1)S(1)}, bf16[16,768]{1,0:T(8,128)(2,1)S(1)}) custom-call(bf16[64,128]{1,0:T(8,128)(2,1)S(1)} %bitcast.13, f32[2]{0:T(128)S(1)} %copy-done.9, s32[1]{0:T(128)S(6)} %copy.20.psf_of_ref, bf16[4,2,2,48,768]{4,3,2,1,0:T(8,128)(2,1)S(1)} %copy-done, ...), custom_call_target="tpu_custom_call" | custom-call | tf_op jit(solution)/shard_map/exchange/pallas_call | solution.py:219
  48.6 0.0 copy-done.6
  48.6 0.0 copy-start.1
  48.6 1.3 %copy-done.1 = bf16[4,2,2,48,768]{4,3,2,1,0:T(8,128)(2,1)S(1)} copy-done((bf16[4,2,2,48,768]{4,3,2,1,0:T(8,128)(2,1)S(1)}, bf16[4,2,2,48,768]{4,3,2,1,0:T(8,128)(2,1)}, u32[]{:S(2)}) %copy-start.1) | copy-done | bytes 1179672
  49.9 0.0 copy-start.4
  49.9 1.3 %copy-done.4 = bf16[768,768]{1,0:T(8,128)(2,1)S(1)} copy-done((bf16[768,768]{1,0:T(8,128)(2,1)S(1)}, bf16[768,768]{1,0:T(8,128)(2,1)}, u32[]{:S(2)}) %copy-start.4) | copy-done | bytes 1179672
  51.1 0.0 copy-start.2
  51.2 5.8 %products.1.prod_ref = bf16[16,48,1536]{2,1,0:T(8,128)(2,1)S(1)} custom-call(s32[4,2]{1,0:T(4,128)S(1)} %copy.18.tile_pos_ref, bf16[16,80,128]{2,1,0:T(8,128)(2,1)S(1)} %get-tuple-element.8.model_ref, bf16[4,2,2,48,768]{4,3,2,1,0:T(8,128)(2,1)S(1)} %copy-done.1, bf16[8,48,768]{2,1,0:T(8,128)(2,1)S(1)} %get-tuple-element.9.far_ref, ...), custom_call_target="tpu_custom_call" | custom-call | tf_op jit(solution)/shard_map/products/pallas_call | solution.py:344
  57.0 0.0 copy-done.2
  57.0 0.0 copy-start.3
  57.0 0.0 copy-start.5
  57.0 24.4 %columns.1 = bf16[2,16,48,512]{3,2,1,0:T(8,128)(2,1)S(1)} custom-call(bf16[16,48,1536]{2,1,0:T(8,128)(2,1)S(1)} %products.1.prod_ref, bf16[1536,1024]{1,0:T(8,128)(2,1)S(1)} %copy-done.2), custom_call_target="tpu_custom_call" | custom-call | tf_op jit(solution)/shard_map/columns/pallas_call | solution.py:410
  81.4 0.0 copy-done.3
  81.4 0.0 copy-done.5
  81.4 2.2 %subtract.1 = f32[2,1,512,512]{3,2,1,0:T(8,128)} custom-call(f32[2,1,512,512]{3,2,1,0:T(8,128)S(1)} %copy-done.3, bf16[2,768,512]{2,1,0:T(8,128)(2,1)S(1)} %bitcast.12, bf16[512,768]{1,0:T(8,128)(2,1)S(1)} %copy-done.5), custom_call_target="tpu_custom_call" | custom-call | tf_op jit(solution)/shard_map/subtract/pallas_call | solution.py:427
  (3 shorter events, 0.0 us)
Async XLA Ops:
  0.0 48.6 %copy-start.6 = (bf16[256,1536]{1,0:T(8,128)(2,1)S(1)}, bf16[256,1536]{1,0:T(8,128)(2,1)}, u32[]{:S(2)}) copy-start(bf16[256,1536]{1,0:T(8,128)(2,1)} %constant.67.clone.cols_ref) | copy-start | bytes 2359300
  6.6 1.3 %copy-start = (bf16[4,2,2,48,768]{4,3,2,1,0:T(8,128)(2,1)S(1)}, bf16[4,2,2,48,768]{4,3,2,1,0:T(8,128)(2,1)}, u32[]{:S(2)}) copy-start(bf16[4,2,2,48,768]{4,3,2,1,0:T(8,128)(2,1)} %psf_ref.3) | copy-start | bytes 3538948
  7.8 0.7 copy-start.7
  8.5 0.7 copy-start.8
  9.2 0.7 copy-start.9
  48.6 1.3 %copy-start.1 = (bf16[4,2,2,48,768]{4,3,2,1,0:T(8,128)(2,1)S(1)}, bf16[4,2,2,48,768]{4,3,2,1,0:T(8,128)(2,1)}, u32[]{:S(2)}) copy-start(bf16[4,2,2,48,768]{4,3,2,1,0:T(8,128)(2,1)} %psf_ref.3) | copy-start | bytes 3538948
  49.9 1.3 %copy-start.4 = (bf16[768,768]{1,0:T(8,128)(2,1)S(1)}, bf16[768,768]{1,0:T(8,128)(2,1)}, u32[]{:S(2)}) copy-start(bf16[768,768]{1,0:T(8,128)(2,1)} %constant.70.clone.flip_ref) | copy-start | bytes 3538948
  51.1 5.9 %copy-start.2 = (bf16[1536,1024]{1,0:T(8,128)(2,1)S(1)}, bf16[1536,1024]{1,0:T(8,128)(2,1)}, u32[]{:S(2)}) copy-start(bf16[1536,1024]{1,0:T(8,128)(2,1)} %constant.68.clone.back_ref) | copy-start | bytes 9437188
  57.0 24.4 %copy-start.3 = (f32[2,1,512,512]{3,2,1,0:T(8,128)S(1)}, f32[2,1,512,512]{3,2,1,0:T(8,128)}, u32[]{:S(2)}) copy-start(f32[2,1,512,512]{3,2,1,0:T(8,128)} %residual_ref.1) | copy-start | bytes 6291460
  57.0 24.4 %copy-start.5 = (bf16[512,768]{1,0:T(8,128)(2,1)S(1)}, bf16[512,768]{1,0:T(8,128)(2,1)}, u32[]{:S(2)}) copy-start(bf16[512,768]{1,0:T(8,128)(2,1)} %constant.69.clone.back_ref) | copy-start | bytes 2359300
where the time goes:
time: 84.1 us; the launch traced here: 83.6 us
  Pallas kernels  71 us (84%)
  local copies, waits for them, and re-layouts  11 us (13%)
  between operations  0.85 us (1%)
    pallas_call x1, Pallas kernels, exchange(): pl.pallas_call(exchange_kernel, out_shape=(jax.ShapeDtypeStruct((N, 80, 1...  38.7 us
    pallas_call x1, Pallas kernels, columns(): pl.pallas_call(columns_kernel, out_shape=jax.ShapeDtypeStruct((2, N, 48,...  24.4 us
    unnamed x21, local copies, waits for them, and re-layouts  6.66 us
    pallas_call x1, Pallas kernels, products(): pl.pallas_call(product_kernel, out_shape=jax.ShapeDtypeStruct((N, 48, 2 *...  5.84 us
    pallas_call x1, Pallas kernels, subtract(): pl.pallas_call(rows_kernel, grid=(2,), out_shape=jax.ShapeDtypeStruct(res...  2.16 us

commit v1 on v0

v1 whole, which is shorter than its diff:
```python
import functools
import math

import jax
import jax.numpy as jnp
import ml_dtypes
import numpy as np
from jax import lax
from jax.experimental import pallas as pl
from jax.experimental.pallas import tpu as pltpu
from jax.sharding import PartitionSpec as P

CHAN = 32
FS = 512
PAD = 128
TS = 128
NTILE = 4
FCOLS = 4
FRAME = 768
N = 16
ROWS = 48
SLOTS = 24
MIB = 1 << 20
MESH = pl.DeviceIdType.MESH
VMEM = pl.BlockSpec(memory_space=pltpu.VMEM)
HBM = pl.BlockSpec(memory_space=pltpu.HBM)
f32 = jnp.float32
bf16 = jnp.bfloat16


def own_row(m, slot):
    return 0 if slot == 0 and m >= N // 2 else SLOTS + slot


def angles(left, right):
    return (left * right % FRAME).astype(np.float64) * (2.0 * math.pi / FRAME)


def half(table):
    return table.astype(ml_dtypes.bfloat16)


@functools.cache
def tables():
    slot_of = np.arange(4)[:, None, None] * 8 + np.arange(8)[None, None, :]
    slot_of = np.broadcast_to(slot_of, (4, 2, 8)).reshape(-1)
    chan_of = np.broadcast_to(np.arange(2)[None, :, None], (4, 2, 8)).reshape(-1)
    k_rows = np.zeros((N, 64), np.int64)
    own = np.zeros((N, 48, 96))
    mirror = np.zeros((48, 96))
    for m in range(N):
        for r in range(48):
            k_rows[m, r] = ROWS * m + own_row(m, slot_of[r])
            own[m, r, chan_of[r] * ROWS + own_row(m, slot_of[r])] = 1.0
    for r in range(48):
        mirror[r, chan_of[r] * ROWS + SLOTS - slot_of[r]] = 1.0
    tile_rows = np.arange(N)[:, None, None] * 8 + np.arange(8)[None, None, :]
    tile_rows = np.broadcast_to(tile_rows, (N, 2, 8)).reshape(-1)
    tile_chan = np.broadcast_to(np.arange(2)[None, :, None], (N, 2, 8)).reshape(-1)
    theta = angles(k_rows[:, :, None], tile_rows[None, None, :])
    same = (chan_of[:, None] == tile_chan[None, :])[None]
    rows = np.concatenate([np.cos(theta) * same, -np.sin(theta) * same], axis=1)
    theta = angles(np.arange(TS)[:, None], np.arange(FRAME)[None, :])
    cos, sin = np.cos(theta), np.sin(theta)
    cols = np.block([[cos, -sin], [sin, cos]])
    theta = angles(np.arange(FRAME)[:, None], PAD + np.arange(FS)[None, :])
    cos, sin = np.cos(theta), np.sin(theta)
    back_cols = np.block([[cos, sin], [-sin, cos]])
    back_rows = np.zeros((FS, N, 2, SLOTS))
    y = PAD + np.arange(FS)
    for m in range(N):
        for slot in range(SLOTS):
            theta = angles(np.int64(ROWS * m + own_row(m, slot)), y)
            back_rows[:, m, 0, slot] = np.cos(theta)
            back_rows[:, m, 1, slot] = -np.sin(theta)
    back_rows[:, N // 2, 0, 0] *= 0.5
    back_rows[:, N // 2, 1, 0] = 0.5
    flip = np.zeros((FRAME, FRAME))
    flip[(FRAME - np.arange(FRAME)) % FRAME, np.arange(FRAME)] = 1.0
    return dict(
        own=half(own),
        mirror=half(mirror),
        rows=half(rows),
        cols=half(cols),
        back_cols=half(back_cols),
        back_rows=half(back_rows.reshape(FS, N * 2 * SLOTS)),
        flip=half(flip),
    )


def channel_at(index):
    return (2 * index - (CHAN - 1)).astype(f32) * (1.0 / CHAN)


def convolve_kernel(
    comps_hbm, weight_hbm, psf_of_hbm, tile_pos_hbm, psf_hbm, mirror_hbm, own_hbm, rows_hbm, cols_hbm, flip_hbm, back_hbm,
    out_ref,
    comps, weight, psf_own, tile_pos, psf, mirror, own, rows, cols, flip, back,
    send_a, recv_a, send_b, model, send_f, psf_of, send_0, far_0, send_m, far,
    psf_sum, turned, row_ph, col_ph, tiles, shifted, prod, send_w,
    local, send_sems, recv_sems, pair_sems,
):
    facet = lax.axis_index("facet")
    freq = lax.axis_index("freq")
    middle = facet == N // 2
    upper = facet >= N // 2
    barrier = pltpu.get_barrier_semaphore()

    def greet(d, _):
        pl.semaphore_signal(barrier, inc=1, device_id={"freq": (freq + d) % N}, device_id_type=MESH)
        pl.semaphore_signal(barrier, inc=1, device_id={"facet": (facet + d) % N}, device_id_type=MESH)
        return 0

    lax.fori_loop(1, N, greet, 0)
    sources = (
        comps_hbm, weight_hbm, psf_of_hbm, psf_hbm, mirror_hbm, tile_pos_hbm,
        own_hbm.at[facet], rows_hbm.at[facet], flip_hbm, cols_hbm, back_hbm,
    )
    targets = (comps, weight, psf_own, psf, mirror, tile_pos, own, rows, flip, cols, back)
    loads = [pltpu.make_async_copy(*pair, local.at[at]) for at, pair in enumerate(zip(sources, targets))]
    for load in loads:
        load.start()

    def copies(at, axis, source, target):
        me = facet if axis == "facet" else freq

        def copy(d, slot):
            return pltpu.make_async_remote_copy(
                src_ref=source, dst_ref=target.at[slot],
                send_sem=send_sems.at[at, d], recv_sem=recv_sems.at[at, slot],
                device_id={axis: (me + d) % N}, device_id_type=MESH,
            )

        def start(d, _):
            copy(d, me).start()
            return 0

        def land(d, _):
            copy(d, (me + N - d) % N).wait_recv()
            return 0

        def leave(d, _):
            copy(d, me).wait_send()
            return 0

        return tuple(functools.partial(lax.fori_loop, 1, N, step, 0) for step in (start, land, leave))

    start_a, land_a, leave_a = copies(0, "freq", send_a, recv_a)
    start_b, land_b, leave_b = copies(1, "facet", send_b, model)
    start_f, land_f, leave_f = copies(2, "facet", send_f, psf_of)

    for load in loads[:3]:
        load.wait()
    send_a[0:64, :] = comps[...]
    row = lax.broadcasted_iota(jnp.int32, (8, 128), 0)
    parts = []
    for c in range(2):
        whole = jnp.full((8, 128), weight[c], f32)
        first = whole.astype(bf16).astype(f32)
        second = (whole - first).astype(bf16).astype(f32)
        third = (whole - first) - second
        parts.append(jnp.where(row == 0, first, jnp.where(row == 1, second, jnp.where(row == 2, third, 0.0))))
    send_a[64:80, :] = jnp.concatenate(parts, axis=0).astype(bf16)
    send_f[...] = jnp.full((16, 128), psf_own[0].astype(f32), f32).astype(bf16)
    recv_a[freq] = send_a[...]
    psf_of[facet] = send_f[...]
    pl.semaphore_wait(barrier, 2 * (N - 1))
    start_a()

    loads[3].wait()
    loads[4].wait()
    for index in range(8):
        both = psf[index // 2, :, index % 2].reshape(2 * ROWS, FRAME)
        send_m[index] = jnp.dot(mirror[...], both, preferred_element_type=f32).astype(bf16)
    copy_m = pltpu.make_async_remote_copy(
        src_ref=send_m, dst_ref=far, send_sem=pair_sems.at[0], recv_sem=pair_sems.at[1],
        device_id={"facet": N - 1 - facet}, device_id_type=MESH,
    )
    copy_m.start()
    send_0[...] = jnp.concatenate(
        [psf[n // 4, n // 2 % 2, n % 2, 0:1].astype(f32) for n in range(16)], axis=0
    ).astype(bf16)
    is_first = 1 - (facet + N - 1) // N
    is_middle = 1 - ((facet + N // 2) % N + N - 1) // N
    copy_0 = pltpu.make_async_remote_copy(
        src_ref=send_0, dst_ref=far_0, send_sem=pair_sems.at[2], recv_sem=pair_sems.at[3],
        device_id={"facet": (N - facet) % N + (N // 2) * (is_first - is_middle)}, device_id_type=MESH,
    )
    copy_0.start()
    start_f()

    for load in loads[5:]:
        load.wait()
    for index in range(8):
        both = psf[index // 2, :, index % 2].reshape(2 * ROWS, FRAME)
        psf_sum[index // 2, index % 2, 0:48] = jnp.dot(own[...], both, preferred_element_type=f32)
    row_ph[...], col_ph[...] = phases(facet, tile_pos)

    land_a()

    def add(q, total):
        total = list(total)
        block = recv_a[q].astype(f32)
        comp = block[0:64].reshape(NTILE, 2, 8, 128)
        for c in range(2):
            x = channel_at(2 * q + c)
            power = jnp.sum(block[64 + 8 * c : 72 + 8 * c], axis=0, keepdims=True)
            for n in range(5):
                if n < 3:
                    total[n] = total[n] + power * comp[:, c]
                total[3 + n] = total[3 + n] + power
                power = power * x
        return tuple(total)

    zeros = tuple(jnp.zeros((NTILE, 8, 128), f32) for _ in range(3)) + tuple(jnp.zeros((1, 128), f32) for _ in range(5))
    m0, m1, m2, g0, g1, g2, g3, g4 = lax.fori_loop(0, N, add, zeros)
    c00 = g2 * g4 - g3 * g3
    c01 = g2 * g3 - g1 * g4
    c02 = g1 * g3 - g2 * g2
    c11 = g0 * g4 - g2 * g2
    c12 = g1 * g2 - g0 * g3
    c22 = g0 * g2 - g1 * g1
    det = g0 * c00 + g1 * c01 + g2 * c02
    a0 = ((c00 * m0 + c01 * m1 + c02 * m2) / det).astype(bf16).astype(f32)
    a1 = ((c01 * m0 + c11 * m1 + c12 * m2) / det).astype(bf16).astype(f32)
    a2 = ((c02 * m0 + c12 * m1 + c22 * m2) / det).astype(bf16).astype(f32)
    both = []
    for c in range(2):
        x = channel_at(2 * freq + c)
        both.append(a0 + a1 * x + a2 * (x * x))
    send_b[...] = jnp.stack(both, axis=1).reshape(64, 128).astype(bf16)
    model[facet] = send_b[...]
    start_b()

    land_f()
    copy_0.wait()
    copy_m.wait()
    row = lax.broadcasted_iota(jnp.int32, (16, FRAME), 0)
    for index in range(8):
        p, ri = index // 2, index % 2
        zero_row = [far_0[4 * p + 2 * c + ri : 4 * p + 2 * c + ri + 1].astype(f32) for c in range(2)]
        zero_rows = jnp.where(row == 0, zero_row[0], jnp.where(row == 8, zero_row[1], 0.0))
        psf_sum[p, ri, 48:64] = zero_rows
        lead = jnp.where(
            (row % 8 == 0) & upper,
            jnp.where(middle, psf_sum[p, ri, 0:16], zero_rows),
            far[index, 0:16].astype(f32),
        )
        turned[index, 0:16] = lead.astype(bf16)
        turned[index, 16:48] = far[index, 16:48]
        turned[index, 48:64] = zero_rows.astype(bf16)

    def turn(index, _):
        p, ri = index // 2, index % 2
        flipped = jnp.dot(turned[index], flip[...], preferred_element_type=f32)
        psf_sum[p, ri] = psf_sum[p, ri] + flipped * (1 - 2 * ri).astype(f32)
        return 0

    lax.fori_loop(0, 8, turn, 0)

    land_b()
    for t in range(NTILE):
        block = model[:, 16 * t : 16 * t + 16, :].reshape(256, 128)
        half_way = jnp.dot(rows[...], block, preferred_element_type=f32).astype(bf16)
        half_way = jnp.concatenate([half_way[0:64], half_way[64:128]], axis=1)
        tiles[t] = jnp.dot(half_way, cols[...], preferred_element_type=f32)

    lane = lax.broadcasted_iota(jnp.int32, (64, 128), 1)
    re, im = slice(0, FRAME), slice(FRAME, 2 * FRAME)

    def copy_w(to, slot):
        return pltpu.make_async_remote_copy(
            src_ref=send_w.at[to], dst_ref=out_ref.at[:, slot], send_sem=send_sems.at[3, to], recv_sem=recv_sems.at[3, slot],
            device_id={"facet": to}, device_id_type=MESH,
        )

    def facet_row(step, _):
        a = (facet // FCOLS + (N - 1 - step)) % FCOLS
        for t in range(NTILE):
            rc = jnp.sum(jnp.where(lane == t * FCOLS + a, row_ph[...], 0.0), axis=1, keepdims=True)
            rs = jnp.sum(jnp.where(lane == t * FCOLS + a + 16, row_ph[...], 0.0), axis=1, keepdims=True)
            tr, ti = tiles[t, :, re], tiles[t, :, im]
            shifted[t, :, re] = rc * tr - rs * ti
            shifted[t, :, im] = rc * ti + rs * tr

        for b in range(FCOLS):
            which = jnp.max(psf_of[a * FCOLS + b].astype(f32))
            pick = [jnp.where(which == p, 1.0, 0.0) for p in range(4)]

            def product(g):
                at = slice(16 * g, 16 * g + 16)
                sr = si = hr = hi = 0.0
                for t in range(NTILE):
                    cc = col_ph[0, t * FCOLS + b : t * FCOLS + b + 1]
                    cs = col_ph[1, t * FCOLS + b : t * FCOLS + b + 1]
                    tr, ti = shifted[t, at, re], shifted[t, at, im]
                    sr = sr + (cc * tr - cs * ti)
                    si = si + (cc * ti + cs * tr)
                for p in range(4):
                    hr = hr + pick[p] * psf_sum[p, 0, at]
                    hi = hi + pick[p] * psf_sum[p, 1, at]
                return sr * hr - si * hi, sr * hi + si * hr

            for g in range(3):
                pr, pi = product(g)
                prod[b, 16 * g : 16 * g + 16, re] = pr.astype(bf16)
                prod[b, 16 * g : 16 * g + 16, im] = pi.astype(bf16)

            @pl.when(middle)
            def _():
                pr, pi = product(0)
                more_r, more_i = product(3)
                prod[b, 0:16, re] = (pr - more_i).astype(bf16)
                prod[b, 0:16, im] = (pi + more_r).astype(bf16)

        w = jnp.dot(prod[...].reshape(FCOLS * 48, 2 * FRAME), back[...], preferred_element_type=f32)
        w = w.reshape(FCOLS, 3, 2, 8, 2 * FS)
        for b in range(FCOLS):
            for c in range(2):
                real = w[b, :, c, :, 0:FS].reshape(SLOTS, FS)
                imag = w[b, :, c, :, FS : 2 * FS].reshape(SLOTS, FS)
                send_w[a * FCOLS + b, c] = jnp.concatenate([real, imag], axis=0).astype(bf16)
        for n in range(FCOLS):
            to = a * FCOLS + (facet + n) % FCOLS

            @pl.when(to != facet)
            def _():
                copy_w(to, facet).start()

        return 0

    lax.fori_loop(0, FCOLS, facet_row, 0)
    for c in range(2):
        out_ref[c, facet] = send_w[facet, c]
    leave_a()
    leave_f()
    leave_b()

    def land_w(d, _):
        copy_w((facet + N - d) % N, (facet + N - d) % N).wait()
        return 0

    lax.fori_loop(1, N, land_w, 0)


def phases(facet, tile_pos):
    def turn(index, offset):
        index = index * offset
        theta = (index - jnp.floor(index * (1.0 / FRAME)) * FRAME) * (2.0 * math.pi / FRAME)
        counted = jnp.where((offset >= 0.0) & (offset <= FRAME - TS), 1.0, 0.0)
        return jnp.cos(theta) * counted, -jnp.sin(theta) * counted

    def offsets(place, dim):
        tile = place // FCOLS % NTILE
        at = jnp.zeros(place.shape, jnp.int32)
        for t in range(NTILE):
            at = jnp.where(tile == t, tile_pos[dim, t], at)
        return (at - place % FCOLS * FS + PAD).astype(f32)

    row = lax.broadcasted_iota(jnp.int32, (64, 128), 0)
    lane = lax.broadcasted_iota(jnp.int32, (64, 128), 1)
    slot = row // 16 * 8 + row % 8
    k = facet * ROWS + jnp.where((slot == 0) & (facet >= N // 2), 0, SLOTS + slot)
    k = jnp.where(row >= 48, 0, k).astype(f32)
    cos, sin = turn(k, offsets(lane, 0))
    rows = jnp.where(lane < 16, cos, sin)
    place = lax.broadcasted_iota(jnp.int32, (16, FRAME), 0)
    l = lax.broadcasted_iota(jnp.int32, (16, FRAME), 1).astype(f32)
    return rows, jnp.stack(turn(l, offsets(place, 1)))


def convolve(*args):
    dma = pltpu.SemaphoreType.DMA
    return pl.pallas_call(
        convolve_kernel,
        out_shape=jax.ShapeDtypeStruct((2, N, 48, FS), bf16),
        in_specs=[HBM] * 11,
        out_specs=VMEM,
        scratch_shapes=[
            pltpu.VMEM((64, 128), bf16),
            pltpu.SMEM((2,), f32),
            pltpu.SMEM((1,), jnp.int32),
            pltpu.SMEM((2, NTILE), jnp.int32),
            pltpu.VMEM((4, 2, 2, ROWS, FRAME), bf16),
            pltpu.VMEM((48, 96), bf16),
            pltpu.VMEM((48, 96), bf16),
            pltpu.VMEM((128, 256), bf16),
            pltpu.VMEM((256, 2 * FRAME), bf16),
            pltpu.VMEM((FRAME, FRAME), bf16),
            pltpu.VMEM((2 * FRAME, 2 * FS), bf16),
            pltpu.VMEM((80, 128), bf16),
            pltpu.VMEM((N, 80, 128), bf16),
            pltpu.VMEM((64, 128), bf16),
            pltpu.VMEM((N, 64, 128), bf16),
            pltpu.VMEM((16, 128), bf16),
            pltpu.VMEM((N, 16, 128), bf16),
            pltpu.VMEM((16, FRAME), bf16),
            pltpu.VMEM((16, FRAME), bf16),
            pltpu.VMEM((8, 48, FRAME), bf16),
            pltpu.VMEM((8, 48, FRAME), bf16),
            pltpu.VMEM((4, 2, 64, FRAME), f32),
            pltpu.VMEM((8, 64, FRAME), bf16),
            pltpu.VMEM((64, 128), f32),
            pltpu.VMEM((2, 16, FRAME), f32),
            pltpu.VMEM((NTILE, 64, 2 * FRAME), f32),
            pltpu.VMEM((NTILE, 64, 2 * FRAME), f32),
            pltpu.VMEM((FCOLS, 48, 2 * FRAME), bf16),
            pltpu.VMEM((N, 2, 48, FS), bf16),
            dma((11,)), dma((4, N)), dma((4, N)), dma((4,)),
        ],
        compiler_params=pltpu.CompilerParams(collective_id=0, has_side_effects=True, vmem_limit_bytes=56 * MIB),
        name="convolve",
    )(*args)


def rows_kernel(residual_ref, w_ref, back_ref, out_ref):
    convolved = jnp.dot(back_ref[...], w_ref[0], preferred_element_type=f32)
    out_ref[0, 0] = residual_ref[0, 0] - convolved * (1.0 / (FRAME * FRAME))


def subtract(residual, w, back):
    return pl.pallas_call(
        rows_kernel,
        grid=(2,),
        out_shape=jax.ShapeDtypeStruct(residual.shape, f32),
        in_specs=[
            pl.BlockSpec((1, 1, FS, FS), lambda c: (c, 0, 0, 0)),
            pl.BlockSpec((1, FRAME, FS), lambda c: (c, 0, 0)),
            pl.BlockSpec((FS, FRAME), lambda c: (0, 0)),
        ],
        out_specs=pl.BlockSpec((1, 1, FS, FS), lambda c: (c, 0, 0, 0)),
        compiler_params=pltpu.CompilerParams(vmem_limit_bytes=24 * MIB),
        name="subtract",
    )(residual, w, back)


def shards(residual, components, chan_weight, tile_pos, facet_psf, psf_spectra):
    table = {name: jnp.asarray(value) for name, value in tables().items()}
    w = convolve(
        components.reshape(64, 128), chan_weight, facet_psf, tile_pos.T, psf_spectra,
        *(table[name] for name in ("mirror", "own", "rows", "cols", "flip", "back_cols")),
    )
    return subtract(residual, w.reshape(2, FRAME, FS), table["back_rows"])


def solution(mesh):
    placed = (
        P("freq", "facet", None, None),
        P(None, "freq", "facet", None),
        P("freq"),
        P(),
        P("facet"),
        P(None, "freq", None, "facet", None),
    )
    return jax.shard_map(
        shards,
        mesh=mesh,
        in_specs=placed,
        out_specs=P("freq", "facet", None, None),
        check_vma=False,
    )
```

time: 84.1 us -> 69.8 us (0.83)
  local copies, waits for them, and re-layouts: 11 us -> 1.41 us
  Pallas kernels: 71 us -> 67.6 us
    unnamed x21 -> x6, local copies, waits for them, and re-layouts: 6.66 us -> 1.41 us
    pallas_call x3 -> x1, Pallas kernels: 68.9 us -> 65.5 us  [convolve(): pl.pallas_call(convolve_kernel, out_shape=jax.ShapeDtypeStruct((2, N, 48,...]
    squeeze x2 -> x0, local copies, waits for them, and re-layouts: 1.56 us -> none  [mine(): return lax.dynamic_index_in_dim(table[name], facet, 0, keepdims=False)]
    slice x1 -> x0, local copies, waits for them, and re-layouts: 1.08 us -> none  [shards(): psf_spectra[:, :, :, 0, :].reshape(16, FRAME)]
    sub x3 -> x0, local copies, waits for them, and re-layouts: 0.92 us -> none  [the longest x2 0.84 us: shards(): ox = (tile_pos[:, 1][:, None] - anchors).reshape(-1)]
where the time goes in v1:
time: 69.8 us; the launch traced here: 69.7 us
  Pallas kernels  67.6 us (97%)
  local copies, waits for them, and re-layouts  1.41 us (2%)
  between operations  0.7 us (1%)
    pallas_call x1, Pallas kernels, convolve(): pl.pallas_call(convolve_kernel, out_shape=jax.ShapeDtypeStruct((2, N, 48,...  65.5 us
    pallas_call x1, Pallas kernels, subtract(): pl.pallas_call(rows_kernel, grid=(2,), out_shape=jax.ShapeDtypeStruct(res...  2.13 us
    unnamed x6, local copies, waits for them, and re-layouts  1.41 us

profile of v1, /device:TPU:1, one launch (start us, length us, event | category | flops | bytes accessed | tf_op | source)
XLA Modules:
  0.0 69.7 jit_solution(13089489342460236895)
XLA Ops:
  0.7 0.0 copy-start.1
  0.7 0.0 copy-start.2
  0.7 65.5 %convolve.1 = bf16[2,16,48,512]{3,2,1,0:T(8,128)(2,1)} custom-call(bf16[64,128]{1,0:T(8,128)(2,1)} %bitcast.4, f32[2]{0:T(128)} %weight_hbm.1, s32[1]{0:T(128)S(6)} %copy.14.psf_of_hbm, s32[2,4]{1,0:T(2,128)} %bitcast.5, bf16[4,2,2,48,768]{4,3,2,1,0:T(8,128)(2,1)} %psf_hbm.1, bf16[48,96]{1,0:T(8,128)(2,1)} %constant.15.clone.mirror_hbm, ...), custom_call_target="tpu_custom_call" | custom-call | tf_op jit(solution)/shard_map/convolve/pallas_call | solution.py:374
  66.1 0.0 copy-done.1
  66.1 0.0 copy-done.2
  66.2 0.0 copy-start
  66.2 1.4 %copy-done = bf16[2,16,48,512]{3,2,1,0:T(8,128)(2,1)S(1)} copy-done((bf16[2,16,48,512]{3,2,1,0:T(8,128)(2,1)S(1)}, bf16[2,16,48,512]{3,2,1,0:T(8,128)(2,1)}, u32[]{:S(2)}) %copy-start) | copy-done | bytes 1572888
  67.6 2.1 %subtract.1 = f32[2,1,512,512]{3,2,1,0:T(8,128)} custom-call(f32[2,1,512,512]{3,2,1,0:T(8,128)S(1)} %copy-done.1, bf16[2,768,512]{2,1,0:T(8,128)(2,1)S(1)} %bitcast.3, bf16[512,768]{1,0:T(8,128)(2,1)S(1)} %copy-done.2), custom_call_target="tpu_custom_call" | custom-call | tf_op jit(solution)/shard_map/subtract/pallas_call | solution.py:422
Async XLA Ops:
  0.7 65.5 %copy-start.1 = (f32[2,1,512,512]{3,2,1,0:T(8,128)S(1)}, f32[2,1,512,512]{3,2,1,0:T(8,128)}, u32[]{:S(2)}) copy-start(f32[2,1,512,512]{3,2,1,0:T(8,128)} %residual_ref.1) | copy-start | bytes 6291460
  0.7 65.5 %copy-start.2 = (bf16[512,768]{1,0:T(8,128)(2,1)S(1)}, bf16[512,768]{1,0:T(8,128)(2,1)}, u32[]{:S(2)}) copy-start(bf16[512,768]{1,0:T(8,128)(2,1)} %constant.19.clone.back_ref) | copy-start | bytes 2359300
  66.2 1.4 %copy-start = (bf16[2,16,48,512]{3,2,1,0:T(8,128)(2,1)S(1)}, bf16[2,16,48,512]{3,2,1,0:T(8,128)(2,1)}, u32[]{:S(2)}) copy-start(bf16[2,16,48,512]{3,2,1,0:T(8,128)(2,1)} %convolve.1) | copy-start | bytes 4718596

commit v2 on v1

--- a/solution.py
+++ b/solution.py
@@ -42,18 +42,18 @@
 
 @functools.cache
 def tables():
-    slot_of = np.arange(4)[:, None, None] * 8 + np.arange(8)[None, None, :]
-    slot_of = np.broadcast_to(slot_of, (4, 2, 8)).reshape(-1)
-    chan_of = np.broadcast_to(np.arange(2)[None, :, None], (4, 2, 8)).reshape(-1)
+    chan_of = np.arange(64) // 32
     k_rows = np.zeros((N, 64), np.int64)
     own = np.zeros((N, 48, 96))
     mirror = np.zeros((48, 96))
     for m in range(N):
-        for r in range(48):
-            k_rows[m, r] = ROWS * m + own_row(m, slot_of[r])
-            own[m, r, chan_of[r] * ROWS + own_row(m, slot_of[r])] = 1.0
-    for r in range(48):
-        mirror[r, chan_of[r] * ROWS + SLOTS - slot_of[r]] = 1.0
+        for c in range(2):
+            for slot in range(SLOTS):
+                k_rows[m, 32 * c + slot] = ROWS * m + own_row(m, slot)
+                own[m, SLOTS * c + slot, ROWS * c + own_row(m, slot)] = 1.0
+    for c in range(2):
+        for slot in range(SLOTS):
+            mirror[SLOTS * c + slot, ROWS * c + SLOTS - slot] = 1.0
     tile_rows = np.arange(N)[:, None, None] * 8 + np.arange(8)[None, None, :]
     tile_rows = np.broadcast_to(tile_rows, (N, 2, 8)).reshape(-1)
     tile_chan = np.broadcast_to(np.arange(2)[None, :, None], (N, 2, 8)).reshape(-1)
@@ -113,10 +113,10 @@
 
     lax.fori_loop(1, N, greet, 0)
     sources = (
-        comps_hbm, weight_hbm, psf_of_hbm, psf_hbm, mirror_hbm, tile_pos_hbm,
-        own_hbm.at[facet], rows_hbm.at[facet], flip_hbm, cols_hbm, back_hbm,
-    )
-    targets = (comps, weight, psf_own, psf, mirror, tile_pos, own, rows, flip, cols, back)
+        comps_hbm, weight_hbm, psf_of_hbm, psf_hbm, mirror_hbm, flip_hbm,
+        own_hbm.at[facet], rows_hbm.at[facet], tile_pos_hbm, cols_hbm, back_hbm,
+    )
+    targets = (comps, weight, psf_own, psf, mirror, flip, own, rows, tile_pos, cols, back)
     loads = [pltpu.make_async_copy(*pair, local.at[at]) for at, pair in enumerate(zip(sources, targets))]
     for load in loads:
         load.start()
@@ -164,37 +164,64 @@
     send_f[...] = jnp.full((16, 128), psf_own[0].astype(f32), f32).astype(bf16)
     recv_a[freq] = send_a[...]
     psf_of[facet] = send_f[...]
-    pl.semaphore_wait(barrier, 2 * (N - 1))
-    start_a()
 
     loads[3].wait()
     loads[4].wait()
-    for index in range(8):
-        both = psf[index // 2, :, index % 2].reshape(2 * ROWS, FRAME)
-        send_m[index] = jnp.dot(mirror[...], both, preferred_element_type=f32).astype(bf16)
-    copy_m = pltpu.make_async_remote_copy(
-        src_ref=send_m, dst_ref=far, send_sem=pair_sems.at[0], recv_sem=pair_sems.at[1],
-        device_id={"facet": N - 1 - facet}, device_id_type=MESH,
-    )
-    copy_m.start()
+    loads[5].wait()
+    for p in range(4):
+        parts = [
+            jnp.dot(mirror[...], psf[p, :, ri].reshape(2 * ROWS, FRAME), preferred_element_type=f32) for ri in range(2)
+        ]
+        for c in range(2):
+            part = jnp.concatenate([part[SLOTS * c : SLOTS * (c + 1)] for part in parts], axis=0)
+            turned[c, 48 * p : 48 * (p + 1)] = part.astype(bf16)
+    send_m[...] = (
+        jnp.dot(turned[...].reshape(8 * 48, FRAME), flip[...], preferred_element_type=f32)
+        .astype(bf16)
+        .reshape(2, 4 * 48, FRAME)
+    )
     send_0[...] = jnp.concatenate(
         [psf[n // 4, n // 2 % 2, n % 2, 0:1].astype(f32) for n in range(16)], axis=0
     ).astype(bf16)
+    copies_m = [
+        pltpu.make_async_remote_copy(
+            src_ref=send_m.at[c], dst_ref=far.at[c], send_sem=pair_sems.at[2 + c], recv_sem=pair_sems.at[4 + c],
+            device_id={"facet": N - 1 - facet}, device_id_type=MESH,
+        )
+        for c in range(2)
+    ]
     is_first = 1 - (facet + N - 1) // N
     is_middle = 1 - ((facet + N // 2) % N + N - 1) // N
     copy_0 = pltpu.make_async_remote_copy(
-        src_ref=send_0, dst_ref=far_0, send_sem=pair_sems.at[2], recv_sem=pair_sems.at[3],
+        src_ref=send_0, dst_ref=far_0, send_sem=pair_sems.at[0], recv_sem=pair_sems.at[1],
         device_id={"facet": (N - facet) % N + (N // 2) * (is_first - is_middle)}, device_id_type=MESH,
     )
+    pl.semaphore_wait(barrier, 2 * (N - 1))
+    copies_m[0].start()
+    start_a()
     copy_0.start()
     start_f()
 
-    for load in loads[5:]:
+    for load in loads[6:]:
         load.wait()
     for index in range(8):
         both = psf[index // 2, :, index % 2].reshape(2 * ROWS, FRAME)
-        psf_sum[index // 2, index % 2, 0:48] = jnp.dot(own[...], both, preferred_element_type=f32)
+        chosen = jnp.dot(own[...], both, preferred_element_type=f32)
+        for c in range(2):
+            psf_sum[c, index // 2, index % 2, 0:SLOTS] = chosen[SLOTS * c : SLOTS * (c + 1)]
     row_ph[...], col_ph[...] = phases(facet, tile_pos)
+
+    copy_0.wait()
+    lead_row = lax.broadcasted_iota(jnp.int32, (8, FRAME), 0) == 0
+    zeros_there = far_0[...].astype(f32)
+    ends = jnp.dot(jnp.concatenate([far_0[...], send_0[...]], axis=0), flip[...], preferred_element_type=f32)
+    for n in range(16):
+        p, c, ri = n // 4, n // 2 % 2, n % 2
+        sign = 1.0 - 2.0 * ri
+        there, here = ends[n : n + 1], ends[16 + n : 17 + n]
+        psf_sum[c, p, ri, 24:32] = jnp.where(lead_row, zeros_there[n : n + 1] + sign * there, 0.0)
+        lead = jnp.where(lead_row & upper, jnp.where(middle, here, there), 0.0)
+        psf_sum[c, p, ri, 0:8] = psf_sum[c, p, ri, 0:8] + sign * lead
 
     land_a()
 
@@ -232,63 +259,44 @@
     model[facet] = send_b[...]
     start_b()
 
-    land_f()
-    copy_0.wait()
-    copy_m.wait()
-    row = lax.broadcasted_iota(jnp.int32, (16, FRAME), 0)
-    for index in range(8):
-        p, ri = index // 2, index % 2
-        zero_row = [far_0[4 * p + 2 * c + ri : 4 * p + 2 * c + ri + 1].astype(f32) for c in range(2)]
-        zero_rows = jnp.where(row == 0, zero_row[0], jnp.where(row == 8, zero_row[1], 0.0))
-        psf_sum[p, ri, 48:64] = zero_rows
-        lead = jnp.where(
-            (row % 8 == 0) & upper,
-            jnp.where(middle, psf_sum[p, ri, 0:16], zero_rows),
-            far[index, 0:16].astype(f32),
-        )
-        turned[index, 0:16] = lead.astype(bf16)
-        turned[index, 16:48] = far[index, 16:48]
-        turned[index, 48:64] = zero_rows.astype(bf16)
-
-    def turn(index, _):
-        p, ri = index // 2, index % 2
-        flipped = jnp.dot(turned[index], flip[...], preferred_element_type=f32)
-        psf_sum[p, ri] = psf_sum[p, ri] + flipped * (1 - 2 * ri).astype(f32)
-        return 0
-
-    lax.fori_loop(0, 8, turn, 0)
-
     land_b()
+    copies_m[1].start()
     for t in range(NTILE):
         block = model[:, 16 * t : 16 * t + 16, :].reshape(256, 128)
         half_way = jnp.dot(rows[...], block, preferred_element_type=f32).astype(bf16)
         half_way = jnp.concatenate([half_way[0:64], half_way[64:128]], axis=1)
         tiles[t] = jnp.dot(half_way, cols[...], preferred_element_type=f32)
 
-    lane = lax.broadcasted_iota(jnp.int32, (64, 128), 1)
+    lane = lax.broadcasted_iota(jnp.int32, (32, 128), 1)
     re, im = slice(0, FRAME), slice(FRAME, 2 * FRAME)
 
-    def copy_w(to, slot):
+    def copy_w(c, to, slot):
         return pltpu.make_async_remote_copy(
-            src_ref=send_w.at[to], dst_ref=out_ref.at[:, slot], send_sem=send_sems.at[3, to], recv_sem=recv_sems.at[3, slot],
+            src_ref=send_w.at[c, to], dst_ref=out_ref.at[c, slot],
+            send_sem=send_sems.at[3 + c, to], recv_sem=recv_sems.at[3 + c, slot],
             device_id={"facet": to}, device_id_type=MESH,
         )
 
-    def facet_row(step, _):
+    def facet_row(c, step):
         a = (facet // FCOLS + (N - 1 - step)) % FCOLS
+        base = 32 * c
         for t in range(NTILE):
-            rc = jnp.sum(jnp.where(lane == t * FCOLS + a, row_ph[...], 0.0), axis=1, keepdims=True)
-            rs = jnp.sum(jnp.where(lane == t * FCOLS + a + 16, row_ph[...], 0.0), axis=1, keepdims=True)
-            tr, ti = tiles[t, :, re], tiles[t, :, im]
+            phase = row_ph[base : base + 32]
+            rc = jnp.sum(jnp.where(lane == t * FCOLS + a, phase, 0.0), axis=1, keepdims=True)
+            rs = jnp.sum(jnp.where(lane == t * FCOLS + a + 16, phase, 0.0), axis=1, keepdims=True)
+            tr, ti = tiles[t, base : base + 32, re], tiles[t, base : base + 32, im]
             shifted[t, :, re] = rc * tr - rs * ti
             shifted[t, :, im] = rc * ti + rs * tr
 
-        for b in range(FCOLS):
-            which = jnp.max(psf_of[a * FCOLS + b].astype(f32))
-            pick = [jnp.where(which == p, 1.0, 0.0) for p in range(4)]
-
-            def product(g):
-                at = slice(16 * g, 16 * g + 16)
+        for pair in range(2):
+            picks = []
+            for b in (2 * pair, 2 * pair + 1):
+                which = jnp.max(psf_of[a * FCOLS + b].astype(f32))
+                picks.append([jnp.where(which == p, 1.0, 0.0) for p in range(4)])
+
+            def product(half, g):
+                b = 2 * pair + half
+                at = slice(8 * g, 8 * g + 8)
                 sr = si = hr = hi = 0.0
                 for t in range(NTILE):
                     cc = col_ph[0, t * FCOLS + b : t * FCOLS + b + 1]
@@ -297,47 +305,65 @@
                     sr = sr + (cc * tr - cs * ti)
                     si = si + (cc * ti + cs * tr)
                 for p in range(4):
-                    hr = hr + pick[p] * psf_sum[p, 0, at]
-                    hi = hi + pick[p] * psf_sum[p, 1, at]
+                    hr = hr + picks[half][p] * psf_sum[c, p, 0, at]
+                    hi = hi + picks[half][p] * psf_sum[c, p, 1, at]
                 return sr * hr - si * hi, sr * hi + si * hr
 
-            for g in range(3):
-                pr, pi = product(g)
-                prod[b, 16 * g : 16 * g + 16, re] = pr.astype(bf16)
-                prod[b, 16 * g : 16 * g + 16, im] = pi.astype(bf16)
+            for n in range(3):
+                low, high = (product((2 * n + m) // 3, (2 * n + m) % 3) for m in range(2))
+                at = slice(48 * pair + 16 * n, 48 * pair + 16 * n + 16)
+                prod[at, re] = jnp.concatenate([low[0], high[0]], axis=0).astype(bf16)
+                prod[at, im] = jnp.concatenate([low[1], high[1]], axis=0).astype(bf16)
 
             @pl.when(middle)
             def _():
-                pr, pi = product(0)
-                more_r, more_i = product(3)
-                prod[b, 0:16, re] = (pr - more_i).astype(bf16)
-                prod[b, 0:16, im] = (pi + more_r).astype(bf16)
-
-        w = jnp.dot(prod[...].reshape(FCOLS * 48, 2 * FRAME), back[...], preferred_element_type=f32)
-        w = w.reshape(FCOLS, 3, 2, 8, 2 * FS)
+                for half in range(2):
+                    at = slice(48 * pair + 16 * half, 48 * pair + 16 * half + 16)
+                    pr, pi = product(half, 0)
+                    more_r, more_i = product(half, 3)
+                    lead, near = (pr - more_i, pi + more_r), product(0, 1 + half)
+                    low, high = (lead, near) if half == 0 else (near, lead)
+                    prod[at, re] = jnp.concatenate([low[0], high[0]], axis=0).astype(bf16)
+                    prod[at, im] = jnp.concatenate([low[1], high[1]], axis=0).astype(bf16)
+
+        w = jnp.dot(prod[...], back[...], preferred_element_type=f32)
         for b in range(FCOLS):
-            for c in range(2):
-                real = w[b, :, c, :, 0:FS].reshape(SLOTS, FS)
-                imag = w[b, :, c, :, FS : 2 * FS].reshape(SLOTS, FS)
-                send_w[a * FCOLS + b, c] = jnp.concatenate([real, imag], axis=0).astype(bf16)
+            part = w[SLOTS * b : SLOTS * (b + 1)]
+            both = jnp.concatenate([part[:, 0:FS], part[:, FS : 2 * FS]], axis=0)
+            send_w[c, a * FCOLS + b] = both.astype(bf16)
         for n in range(FCOLS):
             to = a * FCOLS + (facet + n) % FCOLS
 
             @pl.when(to != facet)
             def _():
-                copy_w(to, facet).start()
-
-        return 0
-
-    lax.fori_loop(0, FCOLS, facet_row, 0)
+                copy_w(c, to, facet).start()
+
+    land_f()
     for c in range(2):
-        out_ref[c, facet] = send_w[facet, c]
+        copies_m[c].wait()
+        for index in range(8):
+            if index % 2 == 0:
+                values = far[c, 24 * index : 24 * index + 48].astype(f32)
+            value = values[24 * (index % 2) : 24 * (index % 2) + 24]
+            p, ri = index // 2, index % 2
+            sign = 1.0 - 2.0 * ri
+            lead = jnp.where(lead_row & upper, 0.0, value[0:8])
+            psf_sum[c, p, ri, 0:8] = psf_sum[c, p, ri, 0:8] + sign * lead
+            psf_sum[c, p, ri, 8:24] = psf_sum[c, p, ri, 8:24] + sign * value[8:24]
+
+        def row_step(step, _):
+            facet_row(c, step)
+            return 0
+
+        lax.fori_loop(0, FCOLS, row_step, 0)
+        out_ref[c, facet] = send_w[c, facet]
     leave_a()
     leave_f()
     leave_b()
 
     def land_w(d, _):
-        copy_w((facet + N - d) % N, (facet + N - d) % N).wait()
+        for c in range(2):
+            copy_w(c, (facet + N - d) % N, (facet + N - d) % N).wait()
         return 0
 
     lax.fori_loop(1, N, land_w, 0)
@@ -359,9 +385,9 @@
 
     row = lax.broadcasted_iota(jnp.int32, (64, 128), 0)
     lane = lax.broadcasted_iota(jnp.int32, (64, 128), 1)
-    slot = row // 16 * 8 + row % 8
+    slot = row % 32
     k = facet * ROWS + jnp.where((slot == 0) & (facet >= N // 2), 0, SLOTS + slot)
-    k = jnp.where(row >= 48, 0, k).astype(f32)
+    k = jnp.where(slot >= SLOTS, 0, k).astype(f32)
     cos, sin = turn(k, offsets(lane, 0))
     rows = jnp.where(lane < 16, cos, sin)
     place = lax.broadcasted_iota(jnp.int32, (16, FRAME), 0)
@@ -396,17 +422,17 @@
             pltpu.VMEM((N, 16, 128), bf16),
             pltpu.VMEM((16, FRAME), bf16),
             pltpu.VMEM((16, FRAME), bf16),
-            pltpu.VMEM((8, 48, FRAME), bf16),
-            pltpu.VMEM((8, 48, FRAME), bf16),
-            pltpu.VMEM((4, 2, 64, FRAME), f32),
-            pltpu.VMEM((8, 64, FRAME), bf16),
+            pltpu.VMEM((2, 4 * 48, FRAME), bf16),
+            pltpu.VMEM((2, 4 * 48, FRAME), bf16),
+            pltpu.VMEM((2, 4, 2, 32, FRAME), f32),
+            pltpu.VMEM((2, 4 * 48, FRAME), bf16),
             pltpu.VMEM((64, 128), f32),
             pltpu.VMEM((2, 16, FRAME), f32),
             pltpu.VMEM((NTILE, 64, 2 * FRAME), f32),
-            pltpu.VMEM((NTILE, 64, 2 * FRAME), f32),
-            pltpu.VMEM((FCOLS, 48, 2 * FRAME), bf16),
-            pltpu.VMEM((N, 2, 48, FS), bf16),
-            dma((11,)), dma((4, N)), dma((4, N)), dma((4,)),
+            pltpu.VMEM((NTILE, 32, 2 * FRAME), f32),
+            pltpu.VMEM((FCOLS * SLOTS, 2 * FRAME), bf16),
+            pltpu.VMEM((2, N, 48, FS), bf16),
+            dma((11,)), dma((5, N)), dma((5, N)), dma((6,)),
         ],
         compiler_params=pltpu.CompilerParams(collective_id=0, has_side_effects=True, vmem_limit_bytes=56 * MIB),
         name="convolve",

time: 69.8 us -> 63.4 us (0.908)
  Pallas kernels: 67.6 us -> 61.2 us
    pallas_call x1, Pallas kernels: 65.5 us -> 59.1 us  [convolve(): pl.pallas_call(convolve_kernel, out_shape=jax.ShapeDtypeStruct((2, N, 48,...]
where the time goes in v2:
time: 63.4 us; the launch traced here: 63.3 us
  Pallas kernels  61.2 us (97%)
  local copies, waits for them, and re-layouts  1.41 us (2%)
  between operations  0.7 us (1%)
    pallas_call x1, Pallas kernels, convolve(): pl.pallas_call(convolve_kernel, out_shape=jax.ShapeDtypeStruct((2, N, 48,...  59.1 us
    pallas_call x1, Pallas kernels, subtract(): pl.pallas_call(rows_kernel, grid=(2,), out_shape=jax.ShapeDtypeStruct(res...  2.13 us
    unnamed x6, local copies, waits for them, and re-layouts  1.41 us

profile of v2, /device:TPU:1, one launch (start us, length us, event | category | flops | bytes accessed | tf_op | source)
XLA Modules:
  0.0 63.3 jit_solution(2094763923295703663)
XLA Ops:
  0.7 0.0 copy-start.1
  0.7 0.0 copy-start.2
  0.7 59.1 %convolve.1 = bf16[2,16,48,512]{3,2,1,0:T(8,128)(2,1)} custom-call(bf16[64,128]{1,0:T(8,128)(2,1)} %bitcast.4, f32[2]{0:T(128)} %weight_hbm.1, s32[1]{0:T(128)S(6)} %copy.14.psf_of_hbm, s32[2,4]{1,0:T(2,128)} %bitcast.5, bf16[4,2,2,48,768]{4,3,2,1,0:T(8,128)(2,1)} %psf_hbm.1, bf16[48,96]{1,0:T(8,128)(2,1)} %constant.15.clone.mirror_hbm, ...), custom_call_target="tpu_custom_call" | custom-call | tf_op jit(solution)/shard_map/convolve/pallas_call | solution.py:400
  59.8 0.0 copy-done.1
  59.8 0.0 copy-done.2
  59.8 0.0 copy-start
  59.8 1.4 %copy-done = bf16[2,16,48,512]{3,2,1,0:T(8,128)(2,1)S(1)} copy-done((bf16[2,16,48,512]{3,2,1,0:T(8,128)(2,1)S(1)}, bf16[2,16,48,512]{3,2,1,0:T(8,128)(2,1)}, u32[]{:S(2)}) %copy-start) | copy-done | bytes 1572888
  61.2 2.1 %subtract.1 = f32[2,1,512,512]{3,2,1,0:T(8,128)} custom-call(f32[2,1,512,512]{3,2,1,0:T(8,128)S(1)} %copy-done.1, bf16[2,768,512]{2,1,0:T(8,128)(2,1)S(1)} %bitcast.3, bf16[512,768]{1,0:T(8,128)(2,1)S(1)} %copy-done.2), custom_call_target="tpu_custom_call" | custom-call | tf_op jit(solution)/shard_map/subtract/pallas_call | solution.py:448
Async XLA Ops:
  0.7 59.1 %copy-start.1 = (f32[2,1,512,512]{3,2,1,0:T(8,128)S(1)}, f32[2,1,512,512]{3,2,1,0:T(8,128)}, u32[]{:S(2)}) copy-start(f32[2,1,512,512]{3,2,1,0:T(8,128)} %residual_ref.1) | copy-start | bytes 6291460
  0.7 59.1 %copy-start.2 = (bf16[512,768]{1,0:T(8,128)(2,1)S(1)}, bf16[512,768]{1,0:T(8,128)(2,1)}, u32[]{:S(2)}) copy-start(bf16[512,768]{1,0:T(8,128)(2,1)} %constant.19.clone.back_ref) | copy-start | bytes 2359300
  59.8 1.4 %copy-start = (bf16[2,16,48,512]{3,2,1,0:T(8,128)(2,1)S(1)}, bf16[2,16,48,512]{3,2,1,0:T(8,128)(2,1)}, u32[]{:S(2)}) copy-start(bf16[2,16,48,512]{3,2,1,0:T(8,128)(2,1)} %convolve.1) | copy-start | bytes 4718596

commit v3 on v2

--- a/solution.py
+++ b/solution.py
@@ -19,6 +19,7 @@
 FRAME = 768
 N = 16
 ROWS = 48
+AHEAD = 48
 SLOTS = 24
 MIB = 1 << 20
 MESH = pl.DeviceIdType.MESH
@@ -185,10 +186,13 @@
     ).astype(bf16)
     copies_m = [
         pltpu.make_async_remote_copy(
-            src_ref=send_m.at[c], dst_ref=far.at[c], send_sem=pair_sems.at[2 + c], recv_sem=pair_sems.at[4 + c],
+            src_ref=send_m.at[c, part], dst_ref=far.at[c, part],
+            send_sem=pair_sems.at[2 + at], recv_sem=pair_sems.at[5 + at],
             device_id={"facet": N - 1 - facet}, device_id_type=MESH,
         )
-        for c in range(2)
+        for at, (c, part) in enumerate(
+            ((0, pl.ds(0, 192)), (1, pl.ds(0, AHEAD)), (1, pl.ds(AHEAD, 192 - AHEAD)))
+        )
     ]
     is_first = 1 - (facet + N - 1) // N
     is_middle = 1 - ((facet + N // 2) % N + N - 1) // N
@@ -200,6 +204,7 @@
     copies_m[0].start()
     start_a()
     copy_0.start()
+    copies_m[1].start()
     start_f()
 
     for load in loads[6:]:
@@ -260,7 +265,7 @@
     start_b()
 
     land_b()
-    copies_m[1].start()
+    copies_m[2].start()
     for t in range(NTILE):
         block = model[:, 16 * t : 16 * t + 16, :].reshape(256, 128)
         half_way = jnp.dot(rows[...], block, preferred_element_type=f32).astype(bf16)
@@ -340,7 +345,8 @@
 
     land_f()
     for c in range(2):
-        copies_m[c].wait()
+        for copy_m in copies_m[c : 2 * c + 1]:
+            copy_m.wait()
         for index in range(8):
             if index % 2 == 0:
                 values = far[c, 24 * index : 24 * index + 48].astype(f32)
@@ -432,7 +438,7 @@
             pltpu.VMEM((NTILE, 32, 2 * FRAME), f32),
             pltpu.VMEM((FCOLS * SLOTS, 2 * FRAME), bf16),
             pltpu.VMEM((2, N, 48, FS), bf16),
-            dma((11,)), dma((5, N)), dma((5, N)), dma((6,)),
+            dma((11,)), dma((5, N)), dma((5, N)), dma((8,)),
         ],
         compiler_params=pltpu.CompilerParams(collective_id=0, has_side_effects=True, vmem_limit_bytes=56 * MIB),
         name="convolve",

time: 63.4 us -> 62.5 us (0.986)
  Pallas kernels: 61.2 us -> 60.3 us
    pallas_call x1, Pallas kernels: 59.1 us -> 58.1 us  [convolve(): pl.pallas_call(convolve_kernel, out_shape=jax.ShapeDtypeStruct((2, N, 48,...]
where the time goes in v3:
time: 62.5 us; the launch traced here: 62.4 us
  Pallas kernels  60.3 us (96%)
  local copies, waits for them, and re-layouts  1.41 us (2%)
  between operations  0.7 us (1%)
    pallas_call x1, Pallas kernels, convolve(): pl.pallas_call(convolve_kernel, out_shape=jax.ShapeDtypeStruct((2, N, 48,...  58.1 us
    pallas_call x1, Pallas kernels, subtract(): pl.pallas_call(rows_kernel, grid=(2,), out_shape=jax.ShapeDtypeStruct(res...  2.13 us
    unnamed x6, local copies, waits for them, and re-layouts  1.41 us

profile of v3, /device:TPU:1, one launch (start us, length us, event | category | flops | bytes accessed | tf_op | source)
XLA Modules:
  0.0 62.4 jit_solution(10590459172766294402)
XLA Ops:
  0.7 0.0 copy-start.1
  0.7 0.0 copy-start.2
  0.7 58.1 %convolve.1 = bf16[2,16,48,512]{3,2,1,0:T(8,128)(2,1)} custom-call(bf16[64,128]{1,0:T(8,128)(2,1)} %bitcast.4, f32[2]{0:T(128)} %weight_hbm.1, s32[1]{0:T(128)S(6)} %copy.14.psf_of_hbm, s32[2,4]{1,0:T(2,128)} %bitcast.5, bf16[4,2,2,48,768]{4,3,2,1,0:T(8,128)(2,1)} %psf_hbm.1, bf16[48,96]{1,0:T(8,128)(2,1)} %constant.15.clone.mirror_hbm, ...), custom_call_target="tpu_custom_call" | custom-call | tf_op jit(solution)/shard_map/convolve/pallas_call | solution.py:406
  58.8 0.0 copy-done.1
  58.8 0.0 copy-done.2
  58.8 0.0 copy-start
  58.8 1.4 %copy-done = bf16[2,16,48,512]{3,2,1,0:T(8,128)(2,1)S(1)} copy-done((bf16[2,16,48,512]{3,2,1,0:T(8,128)(2,1)S(1)}, bf16[2,16,48,512]{3,2,1,0:T(8,128)(2,1)}, u32[]{:S(2)}) %copy-start) | copy-done | bytes 1572888
  60.2 2.1 %subtract.1 = f32[2,1,512,512]{3,2,1,0:T(8,128)} custom-call(f32[2,1,512,512]{3,2,1,0:T(8,128)S(1)} %copy-done.1, bf16[2,768,512]{2,1,0:T(8,128)(2,1)S(1)} %bitcast.3, bf16[512,768]{1,0:T(8,128)(2,1)S(1)} %copy-done.2), custom_call_target="tpu_custom_call" | custom-call | tf_op jit(solution)/shard_map/subtract/pallas_call | solution.py:454
Async XLA Ops:
  0.7 58.2 %copy-start.1 = (f32[2,1,512,512]{3,2,1,0:T(8,128)S(1)}, f32[2,1,512,512]{3,2,1,0:T(8,128)}, u32[]{:S(2)}) copy-start(f32[2,1,512,512]{3,2,1,0:T(8,128)} %residual_ref.1) | copy-start | bytes 6291460
  0.7 58.2 %copy-start.2 = (bf16[512,768]{1,0:T(8,128)(2,1)S(1)}, bf16[512,768]{1,0:T(8,128)(2,1)}, u32[]{:S(2)}) copy-start(bf16[512,768]{1,0:T(8,128)(2,1)} %constant.19.clone.back_ref) | copy-start | bytes 2359300
  58.8 1.4 %copy-start = (bf16[2,16,48,512]{3,2,1,0:T(8,128)(2,1)S(1)}, bf16[2,16,48,512]{3,2,1,0:T(8,128)(2,1)}, u32[]{:S(2)}) copy-start(bf16[2,16,48,512]{3,2,1,0:T(8,128)(2,1)} %convolve.1) | copy-start | bytes 4718596

commit v4 on v3

--- a/solution.py
+++ b/solution.py
@@ -264,6 +264,22 @@
     model[facet] = send_b[...]
     start_b()
 
+    def add_mirror(c):
+        for copy_m in copies_m[c : 2 * c + 1]:
+            copy_m.wait()
+        for index in range(8):
+            if index % 2 == 0:
+                values = far[c, 24 * index : 24 * index + 48].astype(f32)
+            value = values[24 * (index % 2) : 24 * (index % 2) + 24]
+            p, ri = index // 2, index % 2
+            sign = 1.0 - 2.0 * ri
+            lead = jnp.where(lead_row & upper, 0.0, value[0:8])
+            psf_sum[c, p, ri, 0:8] = psf_sum[c, p, ri, 0:8] + sign * lead
+            psf_sum[c, p, ri, 8:24] = psf_sum[c, p, ri, 8:24] + sign * value[8:24]
+
+    land_f()
+    add_mirror(0)
+
     land_b()
     copies_m[2].start()
     for t in range(NTILE):
@@ -343,19 +359,9 @@
             def _():
                 copy_w(c, to, facet).start()
 
-    land_f()
     for c in range(2):
-        for copy_m in copies_m[c : 2 * c + 1]:
-            copy_m.wait()
-        for index in range(8):
-            if index % 2 == 0:
-                values = far[c, 24 * index : 24 * index + 48].astype(f32)
-            value = values[24 * (index % 2) : 24 * (index % 2) + 24]
-            p, ri = index // 2, index % 2
-            sign = 1.0 - 2.0 * ri
-            lead = jnp.where(lead_row & upper, 0.0, value[0:8])
-            psf_sum[c, p, ri, 0:8] = psf_sum[c, p, ri, 0:8] + sign * lead
-            psf_sum[c, p, ri, 8:24] = psf_sum[c, p, ri, 8:24] + sign * value[8:24]
+        if c > 0:
+            add_mirror(c)
 
         def row_step(step, _):
             facet_row(c, step)

time: 62.5 us -> 62.3 us (level)
  no operation moved by 1% of the time
where the time goes in v4:
time: 62.3 us; the launch traced here: 62.2 us
  Pallas kernels  60 us (96%)
  local copies, waits for them, and re-layouts  1.41 us (2%)
  between operations  0.7 us (1%)
    pallas_call x1, Pallas kernels, convolve(): pl.pallas_call(convolve_kernel, out_shape=jax.ShapeDtypeStruct((2, N, 48,...  57.9 us
    pallas_call x1, Pallas kernels, subtract(): pl.pallas_call(rows_kernel, grid=(2,), out_shape=jax.ShapeDtypeStruct(res...  2.13 us
    unnamed x6, local copies, waits for them, and re-layouts  1.41 us

profile of v4, /device:TPU:1, one launch (start us, length us, event | category | flops | bytes accessed | tf_op | source)
XLA Modules:
  0.0 62.2 jit_solution(16727124230705372102)
XLA Ops:
  0.7 0.0 copy-start.1
  0.7 0.0 copy-start.2
  0.7 57.9 %convolve.1 = bf16[2,16,48,512]{3,2,1,0:T(8,128)(2,1)} custom-call(bf16[64,128]{1,0:T(8,128)(2,1)} %bitcast.4, f32[2]{0:T(128)} %weight_hbm.1, s32[1]{0:T(128)S(6)} %copy.14.psf_of_hbm, s32[2,4]{1,0:T(2,128)} %bitcast.5, bf16[4,2,2,48,768]{4,3,2,1,0:T(8,128)(2,1)} %psf_hbm.1, bf16[48,96]{1,0:T(8,128)(2,1)} %constant.15.clone.mirror_hbm, ...), custom_call_target="tpu_custom_call" | custom-call | tf_op jit(solution)/shard_map/convolve/pallas_call | solution.py:412
  58.6 0.0 copy-done.1
  58.6 0.0 copy-done.2
  58.6 0.0 copy-start
  58.6 1.4 %copy-done = bf16[2,16,48,512]{3,2,1,0:T(8,128)(2,1)S(1)} copy-done((bf16[2,16,48,512]{3,2,1,0:T(8,128)(2,1)S(1)}, bf16[2,16,48,512]{3,2,1,0:T(8,128)(2,1)}, u32[]{:S(2)}) %copy-start) | copy-done | bytes 1572888
  60.0 2.1 %subtract.1 = f32[2,1,512,512]{3,2,1,0:T(8,128)} custom-call(f32[2,1,512,512]{3,2,1,0:T(8,128)S(1)} %copy-done.1, bf16[2,768,512]{2,1,0:T(8,128)(2,1)S(1)} %bitcast.3, bf16[512,768]{1,0:T(8,128)(2,1)S(1)} %copy-done.2), custom_call_target="tpu_custom_call" | custom-call | tf_op jit(solution)/shard_map/subtract/pallas_call | solution.py:460
Async XLA Ops:
  0.7 57.9 %copy-start.1 = (f32[2,1,512,512]{3,2,1,0:T(8,128)S(1)}, f32[2,1,512,512]{3,2,1,0:T(8,128)}, u32[]{:S(2)}) copy-start(f32[2,1,512,512]{3,2,1,0:T(8,128)} %residual_ref.1) | copy-start | bytes 6291460
  0.7 57.9 %copy-start.2 = (bf16[512,768]{1,0:T(8,128)(2,1)S(1)}, bf16[512,768]{1,0:T(8,128)(2,1)}, u32[]{:S(2)}) copy-start(bf16[512,768]{1,0:T(8,128)(2,1)} %constant.19.clone.back_ref) | copy-start | bytes 2359300
  58.6 1.4 %copy-start = (bf16[2,16,48,512]{3,2,1,0:T(8,128)(2,1)S(1)}, bf16[2,16,48,512]{3,2,1,0:T(8,128)(2,1)}, u32[]{:S(2)}) copy-start(bf16[2,16,48,512]{3,2,1,0:T(8,128)(2,1)} %convolve.1) | copy-start | bytes 4718596
